TPU v7x, 32 devices: a whole 2x2x4 slice. The times are simulated.
32 devices in a mesh: dom: 4 (over z), shard: 8 (over y, x, core).
Axes of the slice: x: 2, y: 2, z: 4, core: 2. Of those that a mesh axis runs over, the one named last changes fastest.
Arguments:
- embedding: float32 [4096, 400], P(('dom', 'shard')), may hold values from -0.9 to 0.9
- accumulator: float32 [4096], P(('dom', 'shard')), may hold values from 0.1 to 1
- relation: float32 [16, 400], replicated, may hold values from 0.1 to 1.9
- plan: int32 [4], replicated, may hold values from 0 to 3, as said below
- lhs_index: int32 [49152], P(('dom', 'shard')), may hold values from 0 to 127
- rhs_index: int32 [49152], P(('dom', 'shard')), may hold values from 0 to 127
- rel_index: int32 [49152], P(('dom', 'shard')), may hold values from 0 to 15
- slot_count: int32 [32, 8], P(('dom', 'shard')), may hold values from 1 to 192, as said below
- neg_span: int32 [96], P(('dom', 'shard')), may hold values from 0 to 2
Outputs:
- entity_grad: float32 [4096, 400], P(('dom', 'shard'))
- adagrad_state: float32 [4096], P(('dom', 'shard'))
- relation_grad: float32 [16, 400], replicated
Inputs may be any that keep to these rules, and one draw needn't show every extreme that they name: plan[d] = d XOR m for one m of 1 to 4 - 1, the same for all d. `slot_count`: every row of groups has some full slot.
All inputs are finite; a program needn't handle non-finite values.
Results may differ from a plain program's by a relative error of at most 0.00079.
Values sent between devices are 32-bit elements; how exact they have to be, the bound alone decides.
A program may use at most 64 MiB of HBM per device.

v0:
```python
import jax
import jax.numpy as jnp
from jax import lax
from jax.sharding import PartitionSpec as P

CH = 512


def soft_weights(positive, scores, live_cols):
    masked = jnp.where(live_cols, scores, -jnp.inf)
    row_max = jnp.maximum(positive, jnp.max(masked, axis=1))
    own_term = jnp.exp(positive - row_max)
    others = jnp.exp(masked - row_max[:, None])
    summed = own_term + jnp.sum(others, axis=1)
    return (others / summed[:, None], own_term / summed)


def add_rows(values, first_row, update):
    current = lax.dynamic_slice_in_dim(values, first_row, update.shape[0], 0)
    return lax.dynamic_update_slice_in_dim(values, current + update, first_row, 0)


def edge_grads(lhs_rows, rel_rows, rhs_rows, valid_rows, negatives, block_size):
    block_count = lhs_rows.shape[0] // block_size
    inner = (((1,), (1,)), ((), ()))
    outer = (((0,), (0,)), ((), ()))

    def one_block(block_index, grad_parts):
        grad_lhs, grad_rhs, grad_rel = grad_parts
        first_row = (block_index * block_size).astype(jnp.int32)
        neg_first = negatives[block_index] * block_size
        lhs_here = lax.dynamic_slice_in_dim(lhs_rows, first_row, block_size, 0)
        rhs_here = lax.dynamic_slice_in_dim(rhs_rows, first_row, block_size, 0)
        rel_here = lax.dynamic_slice_in_dim(rel_rows, first_row, block_size, 0)
        live_here = lax.dynamic_slice_in_dim(valid_rows, first_row, block_size, 0)
        lhs_neg = lax.dynamic_slice_in_dim(lhs_rows, neg_first, block_size, 0).astype(jnp.bfloat16)
        rhs_neg = lax.dynamic_slice_in_dim(rhs_rows, neg_first, block_size, 0).astype(jnp.bfloat16)
        live_neg = lax.dynamic_slice_in_dim(valid_rows, neg_first, block_size, 0)
        left = lhs_here * rel_here
        right = rhs_here * rel_here
        positive = jnp.sum(left * rhs_here, axis=1)
        left_b = left.astype(jnp.bfloat16)
        right_b = right.astype(jnp.bfloat16)
        tail_scores = lax.dot_general(left_b, rhs_neg, inner, preferred_element_type=jnp.float32)
        head_scores = lax.dot_general(right_b, lhs_neg, inner, preferred_element_type=jnp.float32)
        live_cols = live_neg[None, :] > 0.5
        tail_prob, tail_pos = soft_weights(positive, tail_scores, live_cols)
        head_prob, head_pos = soft_weights(positive, head_scores, live_cols)
        weight_pos = live_here * (tail_pos + head_pos - 2.0)
        tail_w = (live_here[:, None] * tail_prob).astype(jnp.bfloat16)
        head_w = (live_here[:, None] * head_prob).astype(jnp.bfloat16)
        grad_left = weight_pos[:, None] * rhs_here + jnp.dot(
            tail_w, rhs_neg, preferred_element_type=jnp.float32
        )
        grad_right = jnp.dot(head_w, lhs_neg, preferred_element_type=jnp.float32)
        grad_lhs = add_rows(grad_lhs, first_row, grad_left * rel_here)
        grad_rhs = add_rows(grad_rhs, first_row, weight_pos[:, None] * left + grad_right * rel_here)
        grad_rel = add_rows(grad_rel, first_row, grad_left * lhs_here + grad_right * rhs_here)
        grad_rhs = add_rows(
            grad_rhs,
            neg_first,
            lax.dot_general(tail_w, left_b, outer, preferred_element_type=jnp.float32),
        )
        grad_lhs = add_rows(
            grad_lhs,
            neg_first,
            lax.dot_general(head_w, right_b, outer, preferred_element_type=jnp.float32),
        )
        return (grad_lhs, grad_rhs, grad_rel)

    empty_grad = jnp.zeros_like(lhs_rows)
    return lax.fori_loop(0, block_count, one_block, (empty_grad, empty_grad, empty_grad))


def pair_move(block_rows, partner):
    row_count = block_rows.shape[0]
    shard_piece = lax.all_gather(block_rows, "dom", axis=0, tiled=True)
    wanted = partner * row_count + jnp.arange(row_count, dtype=jnp.int32)
    inside = (wanted >= 0) & (wanted < shard_piece.shape[0])
    taken = jnp.take(shard_piece, jnp.clip(wanted, 0, shard_piece.shape[0] - 1), axis=0)
    return jnp.where(inside[:, None], taken, 0.0)


def local(
    embedding, accumulator, relation, plan, lhs_index, rhs_index, rel_index, slot_count, neg_span
):
    row_count, width = embedding.shape
    edge_count = lhs_index.shape[0]
    shard_count = lax.axis_size("shard")
    slot_size = edge_count // shard_count
    rel_count = relation.shape[0]
    dom_index = lax.axis_index("dom")
    partner = plan[dom_index]
    partner_rows = pair_move(embedding, partner)
    requests = rhs_index.reshape(shard_count, slot_size)
    asked = lax.all_to_all(requests, "shard", split_axis=0, concat_axis=0, tiled=True)
    served = jnp.take(partner_rows, asked.reshape(-1), axis=0).reshape(
        shard_count, slot_size, width
    )
    rhs_rows = lax.all_to_all(served, "shard", split_axis=0, concat_axis=0, tiled=True).reshape(
        edge_count, width
    )
    lhs_rows = jnp.take(embedding, lhs_index, axis=0)
    rel_onehot = (rel_index[:, None] == jnp.arange(rel_count, dtype=jnp.int32)[None, :]).astype(
        jnp.float32
    )
    rel_rows = jnp.dot(rel_onehot, relation, precision=lax.Precision.HIGHEST)
    live_table = jnp.arange(slot_size, dtype=jnp.int32)[None, :] < slot_count[0][:, None]
    valid_rows = live_table.reshape(edge_count).astype(jnp.float32)
    grad_lhs, grad_rhs, grad_rel = edge_grads(
        lhs_rows, rel_rows, rhs_rows, valid_rows, neg_span, CH
    )
    returned = lax.all_to_all(
        grad_rhs.reshape(shard_count, slot_size, width),
        "shard",
        split_axis=0,
        concat_axis=0,
        tiled=True,
    )
    partner_grad = jax.ops.segment_sum(
        returned.reshape(-1, width), asked.reshape(-1), num_segments=row_count
    )
    own_grad = jax.ops.segment_sum(grad_lhs, lhs_index, num_segments=row_count)
    entity_grad = own_grad + pair_move(partner_grad, partner)
    rel_term = lax.dot_general(
        rel_onehot, grad_rel, (((0,), (0,)), ((), ())), precision=lax.Precision.HIGHEST
    )
    relation_grad = lax.psum(rel_term, ("dom", "shard"))
    adagrad_state = accumulator + jnp.mean(entity_grad * entity_grad, axis=1)
    return (entity_grad, adagrad_state, relation_grad)


def solution(mesh):
    in_specs = (
        P(("dom", "shard"), None),
        P(("dom", "shard")),
        P(),
        P(),
        P(("dom", "shard")),
        P(("dom", "shard")),
        P(("dom", "shard")),
        P(("dom", "shard"), None),
        P(("dom", "shard")),
    )
    out_specs = (P(("dom", "shard"), None), P(("dom", "shard")), P())
    return jax.shard_map(local, mesh=mesh, in_specs=in_specs, out_specs=out_specs, check_vma=False)
```

profile of v0, /device:TPU:0, one launch (start us, length us, event | category | flops | bytes accessed | tf_op | source)
XLA Modules:
  0.0 267.6 jit_solution(13474532359307852321)
XLA Ops:
  2.0 5.2 %all-to-all-start = ((s32[8,1,192]{2,1,0:T(1,128)}), s32[8,1,192]{2,1,0:T(1,128)S(1)}, u32[]{:S(2)}, u32[]{:S(2)}) async-start(s32[8,1,192]{2,1,0:T(1,128)} %all_to_all.12), calls=%async_computation | async-start | bytes 16384 | tf_op jit(solution)/shard_map/all_to_all | solution.py:96
  10.2 22.7 %all_gather.6 = f32[512,400]{1,0:T(8,128)S(1)} all-gather(f32[128,400]{1,0:T(8,128)S(1)} %copy.26), channel_id=1, replica_groups=mesh['dom'=4,'shard'=8] {'dom'}, dimensions={0}, use_global_device_ids=true | all-gather | bytes 1024000 | tf_op jit(solution)/shard_map/all_gather | solution.py:77
  33.9 4.9 %gather_fusion.2 = f32[1536,400]{1,0:T(8,128)} fusion(f32[128,400]{1,0:T(8,128)S(1)} %select_select_fusion.1, s32[2048]{0:T(1024)S(1)} %pad_clamp_fusion), kind=kCustom, calls=%fused_computation.2.clone | custom fusion | bytes 4921344 | tf_op jit(solution)/shard_map/jit(_take)/gather | solution.py:97
  38.8 3.9 %broadcast_select_fusion = f32[1536,400]{1,0:T(8,128)} fusion(f32[1536,400]{1,0:T(8,128)} %gather_fusion.2, pred[1536]{0:T(1024)(128)(4,1)S(1)} %compare_and_fusion), kind=kLoop, calls=%fused_computation.40 | loop fusion | flops 614400 | bytes 4916736 | tf_op jit(solution)/shard_map/jit(_take)/select_n | solution.py:97
  42.7 4.4 %all-to-all-start.1 = ((f32[8,192,400]{2,1,0:T(8,128)}), f32[8,192,400]{2,1,0:T(8,128)S(1)}, u32[]{:S(2)}, u32[]{:S(2)}) async-start(f32[8,192,400]{2,1,0:T(8,128)} %bitcast.3), calls=%async_computation.1 | async-start | bytes 6291456 | tf_op jit(solution)/shard_map/all_to_all | solution.py:100
  47.2 4.9 %gather_fusion = f32[1536,400]{1,0:T(8,128)} fusion(f32[128,400]{1,0:T(8,128)S(1)} %copy.26, s32[2048]{0:T(1024)S(1)} %pad_clamp_fusion.1), kind=kCustom, calls=%fused_computation.clone | custom fusion | bytes 4921344 | tf_op jit(solution)/shard_map/jit(_take)/gather | solution.py:103
  52.1 3.8 %broadcast_select_fusion.1 = f32[1536,400]{1,0:T(8,128)} fusion(f32[1536,400]{1,0:T(8,128)} %gather_fusion, pred[1536]{0:T(1024)(128)(4,1)S(1)} %compare_and_fusion.1), kind=kLoop, calls=%fused_computation.41 | loop fusion | flops 614400 | bytes 4916736 | tf_op jit(solution)/shard_map/jit(_take)/select_n | solution.py:103
  55.9 3.5 %copy.29 = f32[1536,400]{0,1:T(8,128)} copy(f32[1536,400]{1,0:T(8,128)} %broadcast_select_fusion.1) | data formatting | bytes 4915200 | tf_op jit(solution)/shard_map/while | solution.py:72
  59.6 2.8 %fusion.14 = f32[1536,400]{0,1:T(8,128)} fusion(f32[16,400]{1,0:T(8,128)S(1)} %copy-done, s32[1536]{0:T(1024)S(1)} %copy-done.13), kind=kOutput, calls=%fused_computation.44 | convolution fusion | flops 117989376 | bytes 2489344 | tf_op jit(solution)/shard_map/dot_general | solution.py:107
  62.5 22.6 %all-to-all-done.1 = f32[8,192,400]{2,1,0:T(8,128)S(1)} async-done(((f32[8,192,400]{2,1,0:T(8,128)}), f32[8,192,400]{2,1,0:T(8,128)S(1)}, u32[]{:S(2)}, u32[]{:S(2)}) %all-to-all-start.1) | async-done | bytes 2457632 | tf_op jit(solution)/shard_map/all_to_all | solution.py:100
  86.7 2.3 copy.33
  94.3 47.7 %while.19 = (s32[]{:T(128)}, f32[1536,400]{0,1:T(8,128)}, f32[1536,400]{0,1:T(8,128)}, f32[1536,400]{0,1:T(8,128)}, f32[1536]{0:T(1024)S(1)}, /*index=5*/f32[153...) while((s32[]{:T(128)}, f32[1536,400]{0,1:T(8,128)}, ...), condition=%wide.region_6.9_spmd, body=%wide.region_0.8_spmd.sunk | while | flops 1269091840 | bytes 101036032 | solution.py:72
  94.3 2.4 multiply_reduce_fusion.3
  110.2 2.4 multiply_reduce_fusion.3
  126.2 2.4 multiply_reduce_fusion.3
  142.1 3.4 %copy.34 = f32[1536,400]{1,0:T(8,128)} copy(f32[1536,400]{0,1:T(8,128)} %get-tuple-element.227) | data formatting | bytes 4915200 | tf_op jit(solution)/shard_map/reshape | solution.py:114
  145.5 4.6 %all-to-all-start.2 = ((f32[8,192,400]{2,1,0:T(8,128)}), f32[8,192,400]{2,1,0:T(8,128)}, u32[]{:S(2)}, u32[]{:S(2)}) async-start(f32[8,192,400]{2,1,0:T(8,128)} %bitcast.18), calls=%async_computation.2 | async-start | bytes 6291456 | tf_op jit(solution)/shard_map/all_to_all | solution.py:113
  150.1 2.3 copy.31
  152.4 3.2 %fusion.15 = f32[16,400]{1,0:T(8,128)S(1)} fusion(f32[1536,400]{0,1:T(8,128)} %get-tuple-element.229, s32[1536]{0:T(1024)S(1)} %copy-done.13), kind=kOutput, calls=%fused_computation.45 | convolution fusion | flops 118013952 | bytes 2489344 | tf_op jit(solution)/shard_map/dot_general | solution.py:125
  155.6 65.5 %psum.7 = f32[16,400]{1,0:T(8,128)} all-reduce(f32[16,400]{1,0:T(8,128)S(1)} %fusion.15), channel_id=1, replica_groups=mesh['dom'=4,'shard'=8] {'dom','shard'}, use_global_device_ids=true, to_apply=%region_10.13 | all-reduce | flops 6400 | bytes 51200 | tf_op jit(solution)/shard_map/psum | solution.py:128
  221.1 10.3 %scatter_custom_fusion = f32[128,400]{1,0:T(8,128)S(1)} fusion(s32[1536]{0:T(1024)S(1)} %reshape.158, f32[1536,400]{1,0:T(8,128)} %bitcast.6, f32[]{:T(128)} %constant.129.clone.1), kind=kCustom, calls=%fused_computation.51 | custom fusion | flops 614400 | bytes 205312 | tf_op jit(solution)/shard_map/scatter-add | solution.py:120
  231.4 21.1 %all_gather.7 = f32[512,400]{1,0:T(8,128)} all-gather(f32[128,400]{1,0:T(8,128)S(1)} %scatter_custom_fusion), channel_id=1, replica_groups=mesh['dom'=4,'shard'=8] {'dom'}, dimensions={0}, use_global_device_ids=true | all-gather | bytes 1024000 | tf_op jit(solution)/shard_map/all_gather | solution.py:77
  252.5 2.8 %gather_fusion.3 = f32[128,400]{1,0:T(8,128)} fusion(f32[512,400]{1,0:T(8,128)} %all_gather.7, s32[1024]{0:T(1024)S(1)} %pad_clamp_fusion.2), kind=kCustom, calls=%fused_computation.3.clone | custom fusion | bytes 410112 | tf_op jit(solution)/shard_map/jit(_take)/gather | solution.py:80
  256.4 9.8 %scatter_fusion = f32[128,400]{1,0:T(8,128)S(1)} fusion(f32[128,400]{1,0:T(8,128)S(1)} %select_select_fusion, s32[1536]{0:T(1024)S(1)} %copy-done.12, f32[1536,400]{1,0:T(8,128)S(1)} %copy-done.9), kind=kCustom, calls=%fused_computation.5 | custom fusion | flops 614400 | bytes 7378944 | tf_op jit(solution)/shard_map/scatter-add | solution.py:123
  (126 shorter events, 52.8 us)
Async XLA Ops:
  0.6 59.0 %copy-start = (f32[16,400]{1,0:T(8,128)S(1)}, f32[16,400]{1,0:T(8,128)}, u32[]{:S(2)}) copy-start(f32[16,400]{1,0:T(8,128)} %param.17) | copy-start | bytes 76804
  2.0 31.7 %all-to-all-start = ((s32[8,1,192]{2,1,0:T(1,128)}), s32[8,1,192]{2,1,0:T(1,128)S(1)}, u32[]{:S(2)}, u32[]{:S(2)}) async-start(s32[8,1,192]{2,1,0:T(1,128)} %all_to_all.12), calls=%async_computation | async-start | bytes 16384 | tf_op jit(solution)/shard_map/all_to_all | solution.py:96
  42.7 4.4 %copy-start.12 = (s32[1536]{0:T(1024)S(1)}, s32[1536]{0:T(1024)}, u32[]{:S(2)}) copy-start(s32[1536]{0:T(1024)} %param.19) | copy-start | bytes 18436
  42.7 42.3 %all-to-all-start.1 = ((f32[8,192,400]{2,1,0:T(8,128)}), f32[8,192,400]{2,1,0:T(8,128)S(1)}, u32[]{:S(2)}, u32[]{:S(2)}) async-start(f32[8,192,400]{2,1,0:T(8,128)} %bitcast.3), calls=%async_computation.1 | async-start | bytes 6291456 | tf_op jit(solution)/shard_map/all_to_all | solution.py:100
  55.9 3.5 %copy-start.14 = (s32[1,8]{1,0:T(1,128)S(1)}, s32[1,8]{1,0:T(1,128)}, u32[]{:S(2)}) copy-start(s32[1,8]{1,0:T(1,128)} %param.22) | copy-start | bytes 100
  55.9 3.7 %copy-start.13 = (s32[1536]{0:T(1024)S(1)}, s32[1536]{0:T(1024)}, u32[]{:S(2)}) copy-start(s32[1536]{0:T(1024)} %param.21) | copy-start | bytes 18436
  85.0 1.7 copy-start.10
  90.7 3.6 %copy-start.15 = (s32[3]{0:T(128)S(1)}, s32[3]{0:T(128)}, u32[]{:S(2)}) copy-start(s32[3]{0:T(128)} %param.23) | copy-start | bytes 40
  98.5 2.8 %copy-start.7 = (f32[1536,400]{0,1:T(8,128)S(1)}, f32[1536,400]{0,1:T(8,128)}, u32[]{:S(2)}) copy-start(f32[1536,400]{0,1:T(8,128)} %get-tuple-element.412) | copy-start | bytes 7372804 | tf_op jit(solution)/shard_map/while
  100.4 1.7 copy-start.5
  100.8 2.1 copy-start.1
  100.8 2.9 %copy-start.2 = (f32[1536,400]{0,1:T(8,128)S(1)}, f32[1536,400]{0,1:T(8,128)}, u32[]{:S(2)}) copy-start(f32[1536,400]{0,1:T(8,128)} %get-tuple-element.410) | copy-start | bytes 7372804 | tf_op jit(solution)/shard_map/while
  114.4 2.8 %copy-start.7 = (f32[1536,400]{0,1:T(8,128)S(1)}, f32[1536,400]{0,1:T(8,128)}, u32[]{:S(2)}) copy-start(f32[1536,400]{0,1:T(8,128)} %get-tuple-element.412) | copy-start | bytes 7372804 | tf_op jit(solution)/shard_map/while
  116.4 1.7 copy-start.5
  116.8 2.1 copy-start.1
  116.8 2.9 %copy-start.2 = (f32[1536,400]{0,1:T(8,128)S(1)}, f32[1536,400]{0,1:T(8,128)}, u32[]{:S(2)}) copy-start(f32[1536,400]{0,1:T(8,128)} %get-tuple-element.410) | copy-start | bytes 7372804 | tf_op jit(solution)/shard_map/while
  130.3 2.8 %copy-start.7 = (f32[1536,400]{0,1:T(8,128)S(1)}, f32[1536,400]{0,1:T(8,128)}, u32[]{:S(2)}) copy-start(f32[1536,400]{0,1:T(8,128)} %get-tuple-element.412) | copy-start | bytes 7372804 | tf_op jit(solution)/shard_map/while
  132.3 1.7 copy-start.5
  132.7 2.1 copy-start.1
  132.7 2.9 %copy-start.2 = (f32[1536,400]{0,1:T(8,128)S(1)}, f32[1536,400]{0,1:T(8,128)}, u32[]{:S(2)}) copy-start(f32[1536,400]{0,1:T(8,128)} %get-tuple-element.410) | copy-start | bytes 7372804 | tf_op jit(solution)/shard_map/while
  145.5 4.6 %copy-start.4 = (f32[1536,400]{0,1:T(8,128)S(1)}, f32[1536,400]{0,1:T(8,128)}, u32[]{:S(2)}) copy-start(f32[1536,400]{0,1:T(8,128)} %get-tuple-element.228) | copy-start | bytes 7372804
  145.5 75.6 %all-to-all-start.2 = ((f32[8,192,400]{2,1,0:T(8,128)}), f32[8,192,400]{2,1,0:T(8,128)}, u32[]{:S(2)}, u32[]{:S(2)}) async-start(f32[8,192,400]{2,1,0:T(8,128)} %bitcast.18), calls=%async_computation.2 | async-start | bytes 6291456 | tf_op jit(solution)/shard_map/all_to_all | solution.py:113
  155.6 100.7 %copy-start.9 = (f32[1536,400]{1,0:T(8,128)S(1)}, f32[1536,400]{1,0:T(8,128)}, u32[]{:S(2)}) copy-start(f32[1536,400]{1,0:T(8,128)} %copy.31) | copy-start | bytes 7372804
  256.4 10.7 %copy-start.16 = (f32[128]{0:T(128)S(1)}, f32[128]{0:T(128)}, u32[]{:S(2)}) copy-start(f32[128]{0:T(128)} %param.16) | copy-start | bytes 1540
  (12 other events, 17.6 us)
where the time goes:
time: 269 us; the launch traced here: 268 us
  blocking collectives  109 us (41%)
  local copies, waits for them, and re-layouts  56 us (21%)
  other arithmetic  38.2 us (14%)
  matrix products  23.7 us (9%)
  waiting for transfers between devices  22.6 us (8%)
  starting transfers between devices  14.2 us (5%)
    psum x1, blocking collectives, local(): relation_grad = lax.psum(rel_term, ('dom', 'shard'))  65.5 us
    all_gather x2, blocking collectives, pair_move(): shard_piece = lax.all_gather(block_rows, 'dom', axis=0, tiled=True)  43.8 us
    all_to_all x1, waiting for transfers between devices, local(): lax.all_to_all(served, 'shard', split_axis=0, concat_axis=0, tiled=True)  22.6 us
    while x48, local copies, waits for them, and re-layouts  17.6 us
    scatter-add x1, other arithmetic, local(): jax.ops.segment_sum(returned.reshape(-1, width), asked.reshape(-1), num_s...  10.3 us
    scatter-add x1, other arithmetic, local(): own_grad = jax.ops.segment_sum(grad_lhs, lhs_index, num_segments=row_count)  9.77 us
    reduce_sum x3, other arithmetic, one_block(): positive = jnp.sum(left * rhs_here, axis=1)  7.06 us
    dot_general x3, matrix products, one_block(): grad_right = jnp.dot(head_w, lhs_neg, preferred_element_type=jnp.float32)  6.25 us
  transfers between devices with their start and end apart: 3, of which 1 were waited for; matrix products, arithmetic and copies ran while one was open for 9% of the time, Pallas kernels for 0%

commit v1 on v0

v1 whole, which is shorter than its diff:
```python
import functools
import math

import jax
import jax.numpy as jnp
from jax import lax
from jax.experimental import pallas as pl
from jax.experimental.pallas import tpu as pltpu
from jax.sharding import PartitionSpec as P

CH = 512
LANES = 128
MESH = pl.DeviceIdType.MESH
TN = (((0,), (0,)), ((), ()))
NT = (((1,), (1,)), ((), ()))
F32 = jnp.float32
BF16 = jnp.bfloat16


def flip(index, mask):
    out = index
    bit = 1
    while bit <= mask:
        if mask & bit:
            out = out + bit * (1 - 2 * lax.rem(index // bit, 2))
        bit *= 2
    return out


def greet(peers):
    barrier = pltpu.get_barrier_semaphore()
    for peer in peers:
        pl.semaphore_signal(barrier, inc=1, device_id=peer, device_id_type=MESH)
    pl.semaphore_wait(barrier, len(peers))


def send(src, dst, send_sem, recv_sem, peer):
    copy = pltpu.make_async_remote_copy(
        src_ref=src, dst_ref=dst, send_sem=send_sem, recv_sem=recv_sem, device_id=peer, device_id_type=MESH
    )
    copy.start()
    return copy


def fetch_kernel(mask, shards, emb, pack, lhs_out, pack_out, table, own_sem, pair_s, pair_r, chip_s, chip_r, sib_s, sib_r):
    chips = shards // 2
    dom, me = lax.axis_index("dom"), lax.axis_index("shard")
    chip, core = me // 2, lax.rem(me, 2)
    sibling = {"shard": chip * 2 + 1 - core}
    pair = {"dom": flip(dom, mask)}
    others = [{"shard": lax.rem(chip + j, chips) * 2 + core} for j in range(1, chips)]
    own = pltpu.make_async_copy(emb, table.at[me], own_sem)
    own.start()
    greet([sibling, pair] + others)
    moves = [
        send(pack, pack_out, pair_s.at[0], pair_r.at[0], pair),
        send(emb, lhs_out, pair_s.at[1], pair_r.at[1], pair),
    ]
    direct = [send(emb, table.at[me], chip_s.at[j], chip_r.at[j], others[j]) for j in range(chips - 1)]
    moves.append(send(emb, table.at[me], sib_s.at[chips - 1], sib_r.at[chips - 1], sibling))
    for j in range(chips - 1):
        direct[j].wait_recv()
        block = lax.rem(chip + chips - 1 - j, chips) * 2 + core
        moves.append(send(table.at[block], table.at[block], sib_s.at[j], sib_r.at[j], sibling))
    for copy in direct:
        copy.wait_send()
    for copy in moves:
        copy.wait()
    own.wait()


def split(x):
    high = x.astype(BF16)
    return high, (x - high.astype(F32)).astype(BF16)


def dot2(onehot, parts, dims):
    high = lax.dot_general(onehot, parts[0], dims, preferred_element_type=F32)
    return high + lax.dot_general(onehot, parts[1], dims, preferred_element_type=F32)


def edge_kernel(
    shards, slot, meta, pack, lhs_tab, rhs_tab, relation, drhs, dlhs, drel,
    oh_l, oh_r, oh_rel, lhs_s, rhs_s, lhs_b, rhs_b, glhs, grhs, live_col, live_row,
):
    edges = lhs_s.shape[0]
    rows = lhs_tab.shape[0]
    width = lhs_tab.shape[1]
    rels = relation.shape[0]
    subs = edges // LANES
    runs, run_rows, run = oh_r.shape
    owners = run_rows // rows
    spans = edges // CH

    def onehot(number, count):
        ids = lax.broadcasted_iota(jnp.int32, (count, LANES), 0)
        return jnp.where(ids == number, 1.0, 0.0).astype(BF16)

    lane = lax.broadcasted_iota(jnp.int32, (1, LANES), 1)
    for j in range(subs):
        at = slice(j * LANES, (j + 1) * LANES)
        oh_l[:, at] = onehot(pack[j : j + 1, :], rows)
        oh_rel[:, at] = onehot(pack[2 * subs + j : 2 * subs + j + 1, :], rels)
        place = (j * LANES) % run + lane
        shift = jnp.zeros((1, LANES), jnp.int32)
        for g in range(1, owners):
            shift = shift + jnp.where(place >= g * slot, rows, 0)
        inside = (j * LANES) % run
        oh_r[(j * LANES) // run, :, inside : inside + LANES] = onehot(
            pack[subs + j : subs + j + 1, :] + shift, run_rows
        )
    for o in range(shards):
        steps = lax.broadcasted_iota(jnp.int32, (slot, 1), 0)
        live_col[o * slot : (o + 1) * slot, :] = jnp.where(steps < meta[3 * subs, o], 1.0, 0.0)
    for c in range(spans):
        place = c * CH + lax.broadcasted_iota(jnp.int32, (1, CH), 1)
        live = jnp.zeros((1, CH), F32)
        for o in range(c * CH // slot, min(shards, -(-(c + 1) * CH // slot))):
            here = (place >= o * slot) & (place < o * slot + meta[3 * subs, o])
            live = jnp.where(here, 1.0, live)
        live_row[c] = live

    lhs_parts = split(lhs_tab[...])
    rel_parts = split(relation[...])
    for c in range(spans):
        at = slice(c * CH, (c + 1) * CH)
        high = lax.dot_general(oh_l[:, at], lhs_parts[0], TN, preferred_element_type=F32)
        low = lax.dot_general(oh_l[:, at], lhs_parts[1], TN, preferred_element_type=F32)
        lhs_s[at, :] = high + low
        lhs_b[at, :] = high.astype(BF16)
    for t in range(runs):
        at = slice(t * run, (t + 1) * run)
        parts = split(rhs_tab[t * owners : (t + 1) * owners].reshape(run_rows, width))
        high = lax.dot_general(oh_r[t], parts[0], TN, preferred_element_type=F32)
        low = lax.dot_general(oh_r[t], parts[1], TN, preferred_element_type=F32)
        rhs_s[at, :] = high + low
        rhs_b[at, :] = high.astype(BF16)
    glhs[...] = jnp.zeros_like(glhs)
    grhs[...] = jnp.zeros_like(grhs)
    drel[...] = jnp.zeros_like(drel)

    def soft(positive, scores, cols):
        masked = jnp.where(cols, scores, -jnp.inf)
        top = jnp.maximum(positive, jnp.max(masked, axis=1, keepdims=True))
        own = jnp.exp(positive - top)
        others = jnp.exp(masked - top)
        scale = 1.0 / (own + jnp.sum(others, axis=1, keepdims=True))
        return others, own * scale, scale

    def block(c, carry):
        n = meta[3 * subs + 1, c]
        here = pl.ds(pl.multiple_of(c * CH, CH), CH)
        there = pl.ds(pl.multiple_of(n * CH, CH), CH)
        lhs, rhs = lhs_s[here, :], rhs_s[here, :]
        oh = oh_rel[:, here]
        rel = dot2(oh, rel_parts, TN)
        live = live_col[here, :]
        cols = live_row[n] > 0.5
        left, right = lhs * rel, rhs * rel
        positive = jnp.sum(left * rhs, axis=1, keepdims=True)
        left_b, right_b = left.astype(BF16), right.astype(BF16)
        rhs_neg, lhs_neg = rhs_b[there, :], lhs_b[there, :]
        tail = lax.dot_general(left_b, rhs_neg, NT, preferred_element_type=F32)
        head = lax.dot_general(right_b, lhs_neg, NT, preferred_element_type=F32)
        tail, tail_pos, tail_scale = soft(positive, tail, cols)
        head, head_pos, head_scale = soft(positive, head, cols)
        weight = live * (tail_pos + head_pos - 2.0)
        tail_w = (tail * (live * tail_scale)).astype(BF16)
        head_w = (head * (live * head_scale)).astype(BF16)
        grad_left = weight * rhs + jnp.dot(tail_w, rhs_neg, preferred_element_type=F32)
        grad_right = jnp.dot(head_w, lhs_neg, preferred_element_type=F32)
        glhs[here, :] += grad_left * rel
        grhs[here, :] += weight * left + grad_right * rel
        drel[...] += dot2(oh, split(grad_left * lhs + grad_right * rhs), (((1,), (0,)), ((), ())))
        grhs[there, :] += lax.dot_general(tail_w, left_b, TN, preferred_element_type=F32)
        glhs[there, :] += lax.dot_general(head_w, right_b, TN, preferred_element_type=F32)
        return carry

    lax.fori_loop(0, spans, block, 0)
    plain = (((1,), (0,)), ((), ()))
    dlhs[...] = dot2(oh_l[...], split(glhs[...]), plain)
    for t in range(runs):
        sums = dot2(oh_r[t], split(grhs[t * run : (t + 1) * run, :]), plain)
        drhs[t * owners : (t + 1) * owners] = sums.reshape(owners, rows, width)


def return_kernel(
    mask, doms, shards, drhs, dlhs, drel, accumulator, entity, state, rel_out,
    sib_land, sums, land, pair_land, rel_half, rel_sib, rel_sum, rel_chip, rel_sum2, rel_dom, rel_full, rel_back,
    pair_s, pair_r, sib_s, sib_r, chip_s, chip_r, rsib_s, rsib_r, rchip_s, rchip_r, rdom_s, rdom_r, rback_s, rback_r,
):
    chips = shards // 2
    half = rel_half.shape[0]
    dom, me = lax.axis_index("dom"), lax.axis_index("shard")
    chip, core = me // 2, lax.rem(me, 2)
    sibling = {"shard": chip * 2 + 1 - core}
    pair = {"dom": flip(dom, mask)}
    others = [{"shard": lax.rem(chip + j, chips) * 2 + core} for j in range(1, chips)]
    columns = [{"dom": lax.rem(dom + j, doms)} for j in range(1, doms)]
    greet([sibling] + columns + others)

    mine = pl.ds(pl.multiple_of(core * half, half), half)
    yours = pl.ds(pl.multiple_of((1 - core) * half, half), half)
    rel_half[...] = drel[yours, :]
    moves = [send(rel_half, rel_sib, rsib_s, rsib_r, sibling)]
    siblings = []
    for j in range(chips):
        place = lax.rem(chip + (j + 1) % chips, chips) * 2
        siblings.append(send(drhs.at[place + 1 - core], sib_land.at[j], sib_s.at[j], sib_r.at[j], sibling))
    home = send(dlhs, pair_land, pair_s, pair_r, pair)
    moves[0].wait_recv()
    rel_sum[...] = drel[mine, :] + rel_sib[...]
    rel_moves = [send(rel_sum, rel_chip.at[j], rchip_s.at[j], rchip_r.at[j], others[j]) for j in range(chips - 1)]
    directs = []
    for j in range(chips):
        place = lax.rem(chip + (j + 1) % chips, chips) * 2
        siblings[j].wait_recv()
        sums[j] = drhs[place + core] + sib_land[j]
        if j < chips - 1:
            directs.append(send(sums.at[j], land.at[j], chip_s.at[j], chip_r.at[j], others[j]))
    total = rel_sum[...]
    for j in range(chips - 1):
        rel_moves[j].wait_recv()
        total = total + rel_chip[j]
    rel_sum2[...] = total
    dom_moves = [send(rel_sum2, rel_dom.at[j], rdom_s.at[j], rdom_r.at[j], columns[j]) for j in range(doms - 1)]
    total = rel_sum2[...]
    for j in range(doms - 1):
        dom_moves[j].wait_recv()
    total = jnp.zeros_like(total)
    for d in range(doms):
        j = lax.rem(dom + doms - d, doms)
        total = total + jnp.where(j == 0, rel_sum2[...], rel_dom[jnp.maximum(j - 1, 0)])
    rel_full[...] = total
    back = send(rel_full, rel_back, rback_s, rback_r, sibling)
    grads = sums[chips - 1]
    for j in range(chips - 1):
        directs[j].wait_recv()
        grads = grads + land[j]
    home.wait_recv()
    grads = grads + pair_land[...]
    entity[...] = grads
    squares = lax.dot_general(
        jnp.ones((8, grads.shape[1]), F32), grads * grads, NT, precision=lax.Precision.HIGHEST,
        preferred_element_type=F32,
    )
    state[...] = accumulator[...] + squares[0:1, :] / grads.shape[1]
    back.wait_recv()
    rel_out[mine, :] = total
    rel_out[yours, :] = rel_back[...]
    for copy in moves + siblings + [home, back] + rel_moves + directs + dom_moves:
        copy.wait_send()


def local(doms, shards, embedding, accumulator, relation, plan, lhs_index, rhs_index, rel_index, slot_count, neg_span):
    rows, width = embedding.shape
    rels = relation.shape[0]
    edges = lhs_index.shape[0]
    slot = edges // shards
    chips = shards // 2
    spans = edges // CH
    subs = edges // LANES
    run = math.lcm(slot, LANES)
    runs, owners = edges // run, run // slot
    half = rels // 2
    flips = doms - 1
    any_space = pl.BlockSpec(memory_space=pl.ANY)
    vmem = pl.BlockSpec(memory_space=pltpu.VMEM)
    smem = pl.BlockSpec(memory_space=pltpu.SMEM)
    dma = pltpu.SemaphoreType.DMA
    block = jax.ShapeDtypeStruct((rows, width), F32)
    table_type = jax.ShapeDtypeStruct((shards, rows, width), F32)

    pack_rows = -(-(3 * subs + 2) // 8) * 8
    pad = lambda x, size: jnp.pad(x.reshape(-1), (0, size - x.size))
    pack = jnp.concatenate(
        [lhs_index, rhs_index, rel_index, pad(slot_count, LANES), pad(neg_span, (pack_rows - 3 * subs - 1) * LANES)]
    ).reshape(pack_rows, LANES)
    branch = jnp.clip(plan[0] - 1, 0, flips - 1)

    def fetch(mask, emb, pack):
        return pl.pallas_call(
            functools.partial(fetch_kernel, mask, shards),
            out_shape=(block, jax.ShapeDtypeStruct(pack.shape, jnp.int32), table_type),
            in_specs=[any_space] * 2,
            out_specs=(any_space,) * 3,
            scratch_shapes=[
                dma, dma((2,)), dma((2,)), dma((chips - 1,)), dma((chips - 1,)), dma((chips,)), dma((chips,)),
            ],
            compiler_params=pltpu.CompilerParams(collective_id=mask - 1, has_side_effects=True),
            name="fetch_rows",
        )(emb, pack)

    lhs_tab, edges_in, table = lax.switch(
        branch, [functools.partial(fetch, mask) for mask in range(1, doms)], embedding, pack
    )

    drhs, dlhs, drel = pl.pallas_call(
        functools.partial(edge_kernel, shards, slot),
        out_shape=(table_type, block, jax.ShapeDtypeStruct((rels, width), F32)),
        in_specs=[smem] + [vmem] * 4,
        out_specs=(vmem,) * 3,
        scratch_shapes=[
            pltpu.VMEM((rows, edges), BF16),
            pltpu.VMEM((runs, owners * rows, run), BF16),
            pltpu.VMEM((rels, edges), BF16),
            pltpu.VMEM((edges, width), F32),
            pltpu.VMEM((edges, width), F32),
            pltpu.VMEM((edges, width), BF16),
            pltpu.VMEM((edges, width), BF16),
            pltpu.VMEM((edges, width), F32),
            pltpu.VMEM((edges, width), F32),
            pltpu.VMEM((edges, 1), F32),
            pltpu.VMEM((spans, 1, CH), F32),
        ],
        compiler_params=pltpu.CompilerParams(vmem_limit_bytes=56 * 1024 * 1024),
        name="edge_grads",
    )(edges_in, edges_in, lhs_tab, table, relation)

    def give_back(mask, drhs, dlhs, drel, acc):
        small = pltpu.VMEM((half, width), F32)
        return pl.pallas_call(
            functools.partial(return_kernel, mask, doms, shards),
            out_shape=(
                block,
                jax.ShapeDtypeStruct((1, rows), F32),
                jax.ShapeDtypeStruct((rels, width), F32),
            ),
            in_specs=[vmem] * 4,
            out_specs=(vmem,) * 3,
            scratch_shapes=[
                pltpu.VMEM((chips, rows, width), F32),
                pltpu.VMEM((chips, rows, width), F32),
                pltpu.VMEM((chips - 1, rows, width), F32),
                pltpu.VMEM((rows, width), F32),
                small, small, small,
                pltpu.VMEM((chips - 1, half, width), F32),
                small,
                pltpu.VMEM((doms - 1, half, width), F32),
                small, small,
                dma, dma, dma((chips,)), dma((chips,)), dma((chips - 1,)), dma((chips - 1,)),
                dma, dma, dma((chips - 1,)), dma((chips - 1,)), dma((doms - 1,)), dma((doms - 1,)), dma, dma,
            ],
            compiler_params=pltpu.CompilerParams(
                collective_id=flips + mask - 1, has_side_effects=True, vmem_limit_bytes=56 * 1024 * 1024
            ),
            name="return_grads",
        )(drhs, dlhs, drel, acc)

    entity, state, rel_grad = lax.switch(
        branch,
        [functools.partial(give_back, mask) for mask in range(1, doms)],
        drhs, dlhs, drel, accumulator.reshape(1, rows),
    )
    return entity, state.reshape(rows), rel_grad


def solution(mesh):
    both = ("dom", "shard")
    in_specs = (P(both, None), P(both), P(), P(), P(both), P(both), P(both), P(both, None), P(both))
    out_specs = (P(both, None), P(both), P())
    body = functools.partial(local, mesh.shape["dom"], mesh.shape["shard"])
    return jax.shard_map(body, mesh=mesh, in_specs=in_specs, out_specs=out_specs, check_vma=False)
```

time: 269 us -> 63.2 us (0.23)
  blocking collectives: 109 us -> 0 us
  Pallas kernels: 0 us -> 54.4 us
  local copies, waits for them, and re-layouts: 56 us -> 7.15 us
  other arithmetic: 38.2 us -> 0.01 us
  matrix products: 23.7 us -> 0 us
  waiting for transfers between devices: 22.6 us -> 0 us
  starting transfers between devices: 14.2 us -> 0 us
    psum x1 -> x0, blocking collectives: 65.5 us -> none  [local(): relation_grad = lax.psum(rel_term, ('dom', 'shard'))]
    pallas_call x0 -> x3, Pallas kernels: none -> 54.4 us  [the longest x1 20.2 us: fetch(): pl.pallas_call(functools.partial(fetch_kernel, mask, shards), out_shape=(...]
    all_gather x2 -> x0, blocking collectives: 43.8 us -> none  [pair_move(): shard_piece = lax.all_gather(block_rows, 'dom', axis=0, tiled=True)]
    dot_general x20 -> x0, matrix products: 23.7 us -> none  [the longest x3 6.25 us: one_block(): grad_right = jnp.dot(head_w, lhs_neg, preferred_element_type=jnp.float32)]
    while x50 -> x0, local copies, waits for them, and re-layouts: 23.5 us -> none
    all_to_all x3 -> x0, waiting for transfers between devices: 22.6 us -> none  [the longest x1 22.6 us: local(): lax.all_to_all(served, 'shard', split_axis=0, concat_axis=0, tiled=True)]
    scatter-add x2 -> x0, other arithmetic: 20.1 us -> none  [the longest x1 10.3 us: local(): jax.ops.segment_sum(returned.reshape(-1, width), asked.reshape(-1), num_s...]
    all_to_all x3 -> x0, starting transfers between devices: 14.2 us -> none  [the longest x1 5.17 us: local(): lax.all_to_all(requests, 'shard', split_axis=0, concat_axis=0, tiled=True)]
  transfers between devices with their start and end apart: 3 -> 0, of which waited for: 1 -> 0; matrix products, arithmetic and copies ran while one was open for 9% -> 0% of each run, Pallas kernels for 0% -> 0%
where the time goes in v1:
time: 63.2 us; the launch traced here: 62.9 us
  Pallas kernels  54.4 us (86%)
  local copies, waits for them, and re-layouts  7.15 us (11%)
  between operations  1.32 us (2%)
    pallas_call x1, Pallas kernels, fetch(): pl.pallas_call(functools.partial(fetch_kernel, mask, shards), out_shape=(...  20.2 us
    pallas_call x1, Pallas kernels, give_back(): pl.pallas_call(functools.partial(return_kernel, mask, doms, shards), out_...  17.9 us
    pallas_call x1, Pallas kernels, local(): pl.pallas_call(functools.partial(edge_kernel, shards, slot), out_shape=(t...  16.3 us
    unnamed x9, local copies, waits for them, and re-layouts  4.71 us
    another operation x1, local copies, waits for them, and re-layouts  1.77 us

profile of v1, /device:TPU:0, one launch (start us, length us, event | category | flops | bytes accessed | tf_op | source)
XLA Modules:
  0.0 62.9 jit_solution(16159539410570376102)
XLA Ops:
  1.3 0.7 %constant_dynamic-update-slice_fusion.4 = s32[5120]{0:T(1024)S(1)} fusion(s32[5120]{0:T(1024)S(1)} %custom-call, s32[1536]{0:T(1024)} %param.19), kind=kLoop, calls=%fused_computation.4 | loop fusion | bytes 14336
  2.0 0.7 %constant_dynamic-update-slice_fusion.3 = s32[5120]{0:T(1024)S(1)} fusion(s32[5120]{0:T(1024)S(1)} %constant_dynamic-update-slice_fusion.4, s32[1536]{0:T(1024)} %param.20), kind=kLoop, calls=%fused_computation.3 | loop fusion | bytes 14336
  2.7 0.7 %constant_dynamic-update-slice_fusion.2 = s32[5120]{0:T(1024)S(1)} fusion(s32[5120]{0:T(1024)S(1)} %constant_dynamic-update-slice_fusion.3, s32[1536]{0:T(1024)} %param.21), kind=kLoop, calls=%fused_computation.2 | loop fusion | bytes 14336
  3.4 0.7 %constant_dynamic-update-slice_fusion.1 = s32[5120]{0:T(1024)S(1)} fusion(s32[5120]{0:T(1024)S(1)} %constant_dynamic-update-slice_fusion.2, s32[8]{0:T(128)} %bitcast.15), kind=kLoop, calls=%fused_computation.1 | loop fusion | bytes 544
  4.1 0.7 %constant_dynamic-update-slice_fusion = s32[5120]{0:T(1024)S(1)} fusion(s32[5120]{0:T(1024)S(1)} %constant_dynamic-update-slice_fusion.1, s32[3]{0:T(128)} %param.23), kind=kLoop, calls=%fused_computation | loop fusion | bytes 2060 | tf_op jit(solution)/shard_map/concatenate | solution.py:276
  4.7 0.0 copy-start
  4.7 22.0 %conditional.2 = ((f32[128,400]{1,0:T(8,128)S(1)}, s32[40,128]{1,0:T(8,128)S(1)}, f32[8,128,400]{2,1,0:T(8,128)S(1)})) conditional(s32[]{:T(128)} %bitcast.3, (f32[128,400]{0,1:T(8,128)}, s32[40,128]{1,0:T(8,128)S(1)}) %tuple.50, (f32[128,400]{0,1:T(8,128)}, s32[40,128]{1,0:T(8,128)S(1)}) %tuple.51, (f32[128,400]{0,1:T(8,128)}, ...), branch_computations={%region_0.1_spmd, %region_1.2_spmd, %region_2.3_spmd} | conditional | bytes 409608 | solution.py:294
  4.7 1.8 %copy.14.emb = f32[128,400]{1,0:T(8,128)} copy(f32[128,400]{0,1:T(8,128)} %get-tuple-element.98) | data formatting | bytes 409600 | tf_op jit(solution)/shard_map
  6.5 20.2 %fetch_rows.5 = (f32[128,400]{1,0:T(8,128)S(1)}, s32[40,128]{1,0:T(8,128)S(1)}, f32[8,128,400]{2,1,0:T(8,128)S(1)}) custom-call(f32[128,400]{1,0:T(8,128)} %copy.14.emb, s32[40,128]{1,0:T(8,128)S(1)} %get-tuple-element.51.pack), custom_call_target="tpu_custom_call" | custom-call | tf_op jit(solution)/shard_map/cond/branch_2_fun/fetch_rows/pallas_call | solution.py:282
  26.7 16.3 %edge_grads.1 = (f32[8,128,400]{2,1,0:T(8,128)S(1)}, f32[128,400]{1,0:T(8,128)S(1)}, f32[16,400]{1,0:T(8,128)S(1)}) custom-call(s32[40,128]{1,0:T(8,128)S(1)} %get-tuple-element.85.meta.pack, s32[40,128]{1,0:T(8,128)S(1)} %get-tuple-element.85.meta.pack, f32[128,400]{1,0:T(8,128)S(1)} %get-tuple-element.86.lhs_tab, ...), custom_call_target="tpu_custom_call" | custom-call | tf_op jit(solution)/shard_map/edge_grads/pallas_call | solution.py:298
  43.0 0.0 copy-done
  43.0 17.9 %conditional.3 = (f32[128,400]{1,0:T(8,128)S(1)}, f32[16,400]{1,0:T(8,128)S(1)}, f32[128]{0:T(128)S(1)}) conditional(s32[]{:T(128)} %bitcast.3, (f32[8,128,400]{2,1,0:T(8,128)S(1)}, f32[128,400]{1,0:T(8,128)S(1)}, f32[16,400]{1,0:T(8,128)S(1)}, f32[1,128]{1,0:T(1,128)S(1)}) %tuple.53, (f32[8,128,400]{2,1,0:T(8,128)S(1)}, ...), branch_computations={%region_3.4_spmd, %region_4.5_spmd, %region_5.6_spmd} | conditional | bytes 24 | solution.py:350
  43.1 17.9 %return_grads.5 = (f32[128,400]{1,0:T(8,128)S(1)}, f32[1,128]{1,0:T(1,128)S(1)}, f32[16,400]{1,0:T(8,128)S(1)}) custom-call(f32[8,128,400]{2,1,0:T(8,128)S(1)} %get-tuple-element.66.drhs, f32[128,400]{1,0:T(8,128)S(1)} %get-tuple-element.67.dlhs, f32[16,400]{1,0:T(8,128)S(1)} %get-tuple-element.68.drel, f32[1,128]{1,0:T(1,128)S(1)} %get-tuple-element.69.accumulator), custom_call_target="tpu_custom_call" | custom-call | tf_op jit(solution)/shard_map/cond/branch_2_fun/return_grads/pallas_call | solution.py:322
  61.0 0.8 %copy.15 = f32[128,400]{0,1:T(8,128)} copy(f32[128,400]{1,0:T(8,128)S(1)} %get-tuple-element.100) | data formatting | bytes 409600
  61.8 0.5 copy.41
  62.3 0.6 copy.42
  (1 shorter events, 0.0 us)
Async XLA Ops:
  4.7 38.3 %copy-start = (f32[128]{0:T(128)S(1)}, f32[128]{0:T(128)}, u32[]{:S(2)}) copy-start(f32[128]{0:T(128)} %param.16) | copy-start | bytes 1540

commit v2 on v1

v2 whole, which is shorter than its diff:
```python
import functools
import math

import jax
import jax.numpy as jnp
from jax import lax
from jax.experimental import pallas as pl
from jax.experimental.pallas import tpu as pltpu
from jax.sharding import PartitionSpec as P

CH = 512
LANES = 128
MESH = pl.DeviceIdType.MESH
TN = (((0,), (0,)), ((), ()))
NT = (((1,), (1,)), ((), ()))
NN = (((1,), (0,)), ((), ()))
F32 = jnp.float32
BF16 = jnp.bfloat16


def flip(index, mask):
    out = index
    bit = 1
    while bit <= mask:
        if mask & bit:
            out = out + bit * (1 - 2 * lax.rem(index // bit, 2))
        bit *= 2
    return out


def greet(peers):
    barrier = pltpu.get_barrier_semaphore()
    for peer in peers:
        pl.semaphore_signal(barrier, inc=1, device_id=peer, device_id_type=MESH)
    pl.semaphore_wait(barrier, len(peers))


def send(src, dst, send_sem, recv_sem, peer):
    copy = pltpu.make_async_remote_copy(
        src_ref=src, dst_ref=dst, send_sem=send_sem, recv_sem=recv_sem, device_id=peer, device_id_type=MESH
    )
    copy.start()
    return copy


def fetch_kernel(mask, shards, *refs):
    emb, edges_in = refs[0], refs[1:6]
    lhs_out, edges_out, table = refs[6], refs[7:12], refs[12]
    own_sem, pair_s, pair_r, chip_s, chip_r, sib_s, sib_r = refs[13:]
    chips = shards // 2
    dom, me = lax.axis_index("dom"), lax.axis_index("shard")
    chip, core = me // 2, lax.rem(me, 2)
    sibling = {"shard": chip * 2 + 1 - core}
    pair = {"dom": flip(dom, mask)}
    others = [{"shard": lax.rem(chip + j, chips) * 2 + core} for j in range(1, chips)]
    own = pltpu.make_async_copy(emb, table.at[me], own_sem)
    own.start()
    greet([sibling, pair] + others)
    moves = [send(emb, lhs_out, pair_s.at[5], pair_r.at[5], pair)]
    direct = [send(emb, table.at[me], chip_s.at[j], chip_r.at[j], others[j]) for j in range(chips - 1)]
    moves.append(send(emb, table.at[me], sib_s.at[chips - 1], sib_r.at[chips - 1], sibling))
    for i in range(5):
        moves.append(send(edges_in[i], edges_out[i], pair_s.at[i], pair_r.at[i], pair))
    for j in range(chips - 1):
        direct[j].wait_recv()
        block = lax.rem(chip + chips - 1 - j, chips) * 2 + core
        moves.append(send(table.at[block], table.at[block], sib_s.at[j], sib_r.at[j], sibling))
    for copy in direct:
        copy.wait_send()
    for copy in moves:
        copy.wait()
    own.wait()


def split(x):
    high = x.astype(BF16)
    return high, (x - high.astype(F32)).astype(BF16)


def dot(left, right, dims=NN):
    return lax.dot_general(left, right, dims, preferred_element_type=F32)


def edge_kernel(
    shards, slot, counts, negatives, lhs_ids, rhs_ids, rel_ids, lhs_tab, rhs_tab, relation, drhs, dlhs, drel,
    oh_l, oh_r, oh_rel, lhs_s, rhs_s, lhs_b, rhs_b, glhs, grhs, live_col, live_row,
):
    width, rows = lhs_tab.shape
    rels = relation.shape[0]
    spans = lhs_s.shape[0]
    edges = spans * CH
    subs = edges // LANES
    per = CH // LANES
    runs, run_rows, run = oh_r.shape
    owners = run_rows // rows

    def onehot(number, count):
        ids = lax.broadcasted_iota(jnp.int32, (count, LANES), 0)
        return jnp.where(ids == number, 1.0, 0.0).astype(BF16)

    lane = lax.broadcasted_iota(jnp.int32, (1, LANES), 1)
    lhs_rows = lhs_ids[...].reshape(subs, LANES)
    rhs_rows = rhs_ids[...].reshape(subs, LANES)
    rel_rows = rel_ids[...].reshape(subs, LANES)
    for j in range(subs):
        at = slice((j % per) * LANES, (j % per + 1) * LANES)
        oh_l[j // per, :, at] = onehot(lhs_rows[j : j + 1, :], rows)
        oh_rel[j // per, :, at] = onehot(rel_rows[j : j + 1, :], rels)
        inside = (j * LANES) % run
        shift = jnp.zeros((1, LANES), jnp.int32)
        for g in range(1, owners):
            shift = shift + jnp.where(inside + lane >= g * slot, rows, 0)
        oh_r[(j * LANES) // run, :, inside : inside + LANES] = onehot(rhs_rows[j : j + 1, :] + shift, run_rows)
    for o in range(shards):
        steps = lax.broadcasted_iota(jnp.int32, (slot, 1), 0)
        live_col[o * slot : (o + 1) * slot, :] = jnp.where(steps < counts[0, o], 1.0, 0.0)
    for c in range(spans):
        place = c * CH + lax.broadcasted_iota(jnp.int32, (1, CH), 1)
        live = jnp.zeros((1, CH), F32)
        for o in range(c * CH // slot, min(shards, -(-(c + 1) * CH // slot))):
            here = (place >= o * slot) & (place < o * slot + counts[0, o])
            live = jnp.where(here, 1.0, live)
        live_row[c] = live

    lhs_high, lhs_low = split(lhs_tab[...])
    rel_high, rel_low = split(relation[...])
    for c in range(spans):
        high = dot(lhs_high, oh_l[c])
        lhs_s[c] = high + dot(lhs_low, oh_l[c])
        lhs_b[c] = high.astype(BF16)
    for t in range(runs):
        parts = [split(rhs_tab[t * owners + g]) for g in range(owners)]
        high = dot(jnp.concatenate([p[0] for p in parts], axis=1), oh_r[t])
        low = dot(jnp.concatenate([p[1] for p in parts], axis=1), oh_r[t])
        both, high = high + low, high.astype(BF16)
        for i in range(run // LANES):
            k = t * run // LANES + i
            at = slice((k % per) * LANES, (k % per + 1) * LANES)
            rhs_s[k // per, :, at] = both[:, i * LANES : (i + 1) * LANES]
            rhs_b[k // per, :, at] = high[:, i * LANES : (i + 1) * LANES]
    glhs[...] = jnp.zeros_like(glhs)
    grhs[...] = jnp.zeros_like(grhs)

    def soft(positive, scores, live):
        masked = jnp.where(live, scores, -jnp.inf)
        top = jnp.maximum(positive, jnp.max(masked, axis=0, keepdims=True))
        own = jnp.exp(positive - top)
        others = jnp.exp(masked - top)
        scale = 1.0 / (own + jnp.sum(others, axis=0, keepdims=True))
        return others, own * scale, scale

    rel_total = jnp.zeros((rels, width), F32)
    for c in range(spans):
        n = negatives[c]
        lhs, rhs = lhs_s[c], rhs_s[c]
        rel = dot(rel_high, oh_rel[c], TN) + dot(rel_low, oh_rel[c], TN)
        live = live_row[c]
        live_neg = live_col[pl.ds(pl.multiple_of(n * CH, CH), CH), :] > 0.5
        left, right = lhs * rel, rhs * rel
        positive = jnp.sum(left * rhs, axis=0, keepdims=True)
        left_b, right_b = left.astype(BF16), right.astype(BF16)
        rhs_neg, lhs_neg = rhs_b[n], lhs_b[n]
        tail, tail_pos, tail_scale = soft(positive, dot(rhs_neg, left_b, TN), live_neg)
        head, head_pos, head_scale = soft(positive, dot(lhs_neg, right_b, TN), live_neg)
        weight = live * (tail_pos + head_pos - 2.0)
        tail_w = (tail * (live * tail_scale)).astype(BF16)
        head_w = (head * (live * head_scale)).astype(BF16)
        grad_left = weight * rhs + dot(rhs_neg, tail_w)
        grad_right = dot(lhs_neg, head_w)
        glhs[c] += grad_left * rel
        grhs[c] += weight * left + grad_right * rel
        high, low = split(grad_left * lhs + grad_right * rhs)
        rel_total = rel_total + dot(oh_rel[c], high, NT) + dot(oh_rel[c], low, NT)
        grhs[n] += dot(left_b, tail_w, NT)
        glhs[n] += dot(right_b, head_w, NT)
    drel[...] = rel_total

    total = jnp.zeros((width, rows), F32)
    for c in range(spans):
        high, low = split(glhs[c])
        total = total + dot(high, oh_l[c], NT) + dot(low, oh_l[c], NT)
    dlhs[...] = total
    for t in range(runs):
        pieces = []
        for i in range(run // LANES):
            k = t * run // LANES + i
            pieces.append(grhs[k // per, :, (k % per) * LANES : (k % per + 1) * LANES])
        high, low = split(jnp.concatenate(pieces, axis=1))
        sums = dot(high, oh_r[t], NT) + dot(low, oh_r[t], NT)
        for g in range(owners):
            drhs[t * owners + g] = sums[:, g * rows : (g + 1) * rows]


def return_kernel(
    mask, doms, shards, drhs, dlhs, drel, accumulator, entity, state, rel_out,
    sib_land, sums, land, pair_land, rel_half, rel_sib, rel_sum, rel_chip, rel_sum2, rel_dom, rel_full, rel_back,
    pair_s, pair_r, sib_s, sib_r, chip_s, chip_r, rsib_s, rsib_r, rchip_s, rchip_r, rdom_s, rdom_r, rback_s, rback_r,
):
    chips = shards // 2
    half = rel_half.shape[0]
    dom, me = lax.axis_index("dom"), lax.axis_index("shard")
    chip, core = me // 2, lax.rem(me, 2)
    sibling = {"shard": chip * 2 + 1 - core}
    pair = {"dom": flip(dom, mask)}
    others = [{"shard": lax.rem(chip + j, chips) * 2 + core} for j in range(1, chips)]
    columns = [{"dom": lax.rem(dom + j, doms)} for j in range(1, doms)]
    greet([sibling] + columns + others)

    mine = pl.ds(pl.multiple_of(core * half, half), half)
    yours = pl.ds(pl.multiple_of((1 - core) * half, half), half)
    rel_half[...] = drel[yours, :]
    moves = [send(rel_half, rel_sib, rsib_s, rsib_r, sibling)]
    siblings = []
    for j in range(chips):
        place = lax.rem(chip + (j + 1) % chips, chips) * 2
        siblings.append(send(drhs.at[place + 1 - core], sib_land.at[j], sib_s.at[j], sib_r.at[j], sibling))
    home = send(dlhs, pair_land, pair_s, pair_r, pair)
    moves[0].wait_recv()
    rel_sum[...] = drel[mine, :] + rel_sib[...]
    rel_moves = [send(rel_sum, rel_chip.at[j], rchip_s.at[j], rchip_r.at[j], others[j]) for j in range(chips - 1)]
    directs = []
    for j in range(chips):
        place = lax.rem(chip + (j + 1) % chips, chips) * 2
        siblings[j].wait_recv()
        sums[j] = drhs[place + core] + sib_land[j]
        if j < chips - 1:
            directs.append(send(sums.at[j], land.at[j], chip_s.at[j], chip_r.at[j], others[j]))
    total = rel_sum[...]
    for j in range(chips - 1):
        rel_moves[j].wait_recv()
        total = total + rel_chip[j]
    rel_sum2[...] = total
    dom_moves = [send(rel_sum2, rel_dom.at[j], rdom_s.at[j], rdom_r.at[j], columns[j]) for j in range(doms - 1)]
    total = rel_sum2[...]
    for j in range(doms - 1):
        dom_moves[j].wait_recv()
    total = jnp.zeros_like(total)
    for d in range(doms):
        j = lax.rem(dom + doms - d, doms)
        total = total + jnp.where(j == 0, rel_sum2[...], rel_dom[jnp.maximum(j - 1, 0)])
    rel_full[...] = total
    back = send(rel_full, rel_back, rback_s, rback_r, sibling)
    grads = sums[chips - 1]
    for j in range(chips - 1):
        directs[j].wait_recv()
        grads = grads + land[j]
    home.wait_recv()
    grads = grads + pair_land[...]
    entity[...] = grads
    state[...] = accumulator[...] + jnp.sum(grads * grads, axis=0, keepdims=True) / grads.shape[0]
    back.wait_recv()
    rel_out[mine, :] = total
    rel_out[yours, :] = rel_back[...]
    for copy in moves + siblings + [home, back] + rel_moves + directs + dom_moves:
        copy.wait_send()


def local(doms, shards, embedding, accumulator, relation, plan, lhs_index, rhs_index, rel_index, slot_count, neg_span):
    rows, width = embedding.shape
    rels = relation.shape[0]
    edges = lhs_index.shape[0]
    slot = edges // shards
    chips = shards // 2
    spans = edges // CH
    run = math.lcm(slot, LANES)
    runs, owners = edges // run, run // slot
    half = rels // 2
    flips = doms - 1
    any_space = pl.BlockSpec(memory_space=pl.ANY)
    vmem = pl.BlockSpec(memory_space=pltpu.VMEM)
    smem = pl.BlockSpec(memory_space=pltpu.SMEM)
    dma = pltpu.SemaphoreType.DMA
    block = jax.ShapeDtypeStruct((width, rows), F32)
    table_type = jax.ShapeDtypeStruct((shards, width, rows), F32)
    branch = jnp.clip(plan[0] - 1, 0, flips - 1)
    edge_args = (lhs_index, rhs_index, rel_index, slot_count, neg_span)

    def fetch(mask, emb, *edge_args):
        return pl.pallas_call(
            functools.partial(fetch_kernel, mask, shards),
            out_shape=(block,) + tuple(jax.ShapeDtypeStruct(x.shape, x.dtype) for x in edge_args) + (table_type,),
            in_specs=[any_space] * 6,
            out_specs=(any_space,) * 7,
            scratch_shapes=[
                dma, dma((6,)), dma((6,)), dma((chips - 1,)), dma((chips - 1,)), dma((chips,)), dma((chips,)),
            ],
            compiler_params=pltpu.CompilerParams(collective_id=mask - 1, has_side_effects=True),
            name="fetch_rows",
        )(emb, *edge_args)

    lhs_tab, lhs_ids, rhs_ids, rel_ids, counts, negatives, table = lax.switch(
        branch, [functools.partial(fetch, mask) for mask in range(1, doms)], embedding.T, *edge_args
    )

    drhs, dlhs, drel = pl.pallas_call(
        functools.partial(edge_kernel, shards, slot),
        out_shape=(table_type, block, jax.ShapeDtypeStruct((rels, width), F32)),
        in_specs=[smem] * 2 + [vmem] * 6,
        out_specs=(vmem,) * 3,
        scratch_shapes=[
            pltpu.VMEM((spans, rows, CH), BF16),
            pltpu.VMEM((runs, owners * rows, run), BF16),
            pltpu.VMEM((spans, rels, CH), BF16),
            pltpu.VMEM((spans, width, CH), F32),
            pltpu.VMEM((spans, width, CH), F32),
            pltpu.VMEM((spans, width, CH), BF16),
            pltpu.VMEM((spans, width, CH), BF16),
            pltpu.VMEM((spans, width, CH), F32),
            pltpu.VMEM((spans, width, CH), F32),
            pltpu.VMEM((edges, 1), F32),
            pltpu.VMEM((spans, 1, CH), F32),
        ],
        compiler_params=pltpu.CompilerParams(vmem_limit_bytes=56 * 1024 * 1024),
        name="edge_grads",
    )(counts, negatives, lhs_ids, rhs_ids, rel_ids, lhs_tab, table, relation)

    def give_back(mask, drhs, dlhs, drel, acc):
        small = pltpu.VMEM((half, width), F32)
        return pl.pallas_call(
            functools.partial(return_kernel, mask, doms, shards),
            out_shape=(
                block,
                jax.ShapeDtypeStruct((1, rows), F32),
                jax.ShapeDtypeStruct((rels, width), F32),
            ),
            in_specs=[vmem] * 4,
            out_specs=(vmem,) * 3,
            scratch_shapes=[
                pltpu.VMEM((chips, width, rows), F32),
                pltpu.VMEM((chips, width, rows), F32),
                pltpu.VMEM((chips - 1, width, rows), F32),
                pltpu.VMEM((width, rows), F32),
                small, small, small,
                pltpu.VMEM((chips - 1, half, width), F32),
                small,
                pltpu.VMEM((doms - 1, half, width), F32),
                small, small,
                dma, dma, dma((chips,)), dma((chips,)), dma((chips - 1,)), dma((chips - 1,)),
                dma, dma, dma((chips - 1,)), dma((chips - 1,)), dma((doms - 1,)), dma((doms - 1,)), dma, dma,
            ],
            compiler_params=pltpu.CompilerParams(
                collective_id=flips + mask - 1, has_side_effects=True, vmem_limit_bytes=56 * 1024 * 1024
            ),
            name="return_grads",
        )(drhs, dlhs, drel, acc)

    entity, state, rel_grad = lax.switch(
        branch,
        [functools.partial(give_back, mask) for mask in range(1, doms)],
        drhs, dlhs, drel, accumulator.reshape(1, rows),
    )
    return entity.T, state.reshape(rows), rel_grad


def solution(mesh):
    both = ("dom", "shard")
    in_specs = (P(both, None), P(both), P(), P(), P(both), P(both), P(both), P(both, None), P(both))
    out_specs = (P(both, None), P(both), P())
    body = functools.partial(local, mesh.shape["dom"], mesh.shape["shard"])
    return jax.shard_map(body, mesh=mesh, in_specs=in_specs, out_specs=out_specs, check_vma=False)
```

time: 63.2 us -> 49.6 us (0.78)
  Pallas kernels: 54.4 us -> 46.2 us
  local copies, waits for them, and re-layouts: 7.15 us -> 1.81 us
    pallas_call x1, Pallas kernels: 16.3 us -> 13.4 us  [local(): pl.pallas_call(functools.partial(edge_kernel, shards, slot), out_shape=(t...]
    unnamed x9 -> x5, local copies, waits for them, and re-layouts: 4.71 us -> 1.81 us
    pallas_call x1, Pallas kernels: 17.9 us -> 15.2 us  [give_back(): pl.pallas_call(functools.partial(return_kernel, mask, doms, shards), out_...]
    pallas_call x1, Pallas kernels: 20.2 us -> 17.7 us  [fetch(): pl.pallas_call(functools.partial(fetch_kernel, mask, shards), out_shape=(...]
    another operation x1 -> x0, local copies, waits for them, and re-layouts: 1.77 us -> none
    concatenate x1 -> x0, local copies, waits for them, and re-layouts: 0.66 us -> none  [local(): jnp.concatenate([lhs_index, rhs_index, rel_index, pad(slot_count, LANES),...]
where the time goes in v2:
time: 49.6 us; the launch traced here: 49.4 us
  Pallas kernels  46.2 us (93%)
  local copies, waits for them, and re-layouts  1.81 us (4%)
  between operations  1.34 us (3%)
    pallas_call x1, Pallas kernels, fetch(): pl.pallas_call(functools.partial(fetch_kernel, mask, shards), out_shape=(...  17.7 us
    pallas_call x1, Pallas kernels, give_back(): pl.pallas_call(functools.partial(return_kernel, mask, doms, shards), out_...  15.2 us
    pallas_call x1, Pallas kernels, local(): pl.pallas_call(functools.partial(edge_kernel, shards, slot), out_shape=(t...  13.4 us
    unnamed x5, local copies, waits for them, and re-layouts  1.81 us

profile of v2, /device:TPU:0, one launch (start us, length us, event | category | flops | bytes accessed | tf_op | source)
XLA Modules:
  0.0 49.4 jit_solution(4310096842696134393)
XLA Ops:
  0.6 0.0 copy-start
  1.3 17.7 %conditional.2 = ((f32[400,128]{1,0:T(8,128)}, s32[1536]{0:T(1024)S(1)}, s32[1536]{0:T(1024)S(1)}, s32[1536]{0:T(1024)S(1)}, s32[1,8]{1,0:T(1,128)S(1)}, /*index=5*/s32[3]{0:T(128)S(1)}, f32[8,400,128]{2,1,0:T(8,128)S(1)})) conditional(s32[]{:T(128)} %bitcast.3, (f32[400,128]{1,0:T(8,128)}, s32[1536]{0:T(1024)}, s32[1536]{0:T(1024)}, ...), branch_computations={%region_0.1_spmd, %region_1.2_spmd, %region_2.3_spmd} | conditional | bytes 8 | solution.py:291
  1.3 17.7 %fetch_rows.5 = (f32[400,128]{1,0:T(8,128)}, s32[1536]{0:T(1024)S(1)}, s32[1536]{0:T(1024)S(1)}, s32[1536]{0:T(1024)S(1)}, s32[1,8]{1,0:T(1,128)S(1)}, /*index=5*/s32[3]{0:T(128)S(1)}, f32[8,400,128]{2,1,0:T(8,128)S(1)}) custom-call(f32[400,128]{1,0:T(8,128)} %get-tuple-element.82.refs_0_, s32[1536]{0:T(1024)} %get-tuple-element.83.refs_1_, ...), custom_call_target="tpu_custom_call" | custom-call | tf_op jit(solution)/shard_map/cond/branch_2_fun/fetch_rows/pallas_call | solution.py:279
  19.0 13.4 %edge_grads.1 = (f32[8,400,128]{2,1,0:T(8,128)S(1)}, f32[400,128]{1,0:T(8,128)S(1)}, f32[16,400]{1,0:T(8,128)S(1)}) custom-call(s32[1,8]{1,0:T(1,128)S(1)} %get-tuple-element.125.counts, s32[3]{0:T(128)S(1)} %get-tuple-element.126.negatives, s32[1536]{0:T(1024)S(1)} %get-tuple-element.127.lhs_ids, s32[1536]{0:T(1024)S(1)} %get-tuple-element.128.rhs_ids, ...), custom_call_target="tpu_custom_call" | custom-call | tf_op jit(solution)/shard_map/edge_grads/pallas_call | solution.py:295
  32.4 0.0 copy-done
  32.4 15.2 %conditional.3 = (f32[400,128]{1,0:T(8,128)S(1)}, f32[16,400]{1,0:T(8,128)S(1)}, f32[128]{0:T(128)S(1)}) conditional(s32[]{:T(128)} %bitcast.3, (f32[8,400,128]{2,1,0:T(8,128)S(1)}, f32[400,128]{1,0:T(8,128)S(1)}, f32[16,400]{1,0:T(8,128)S(1)}, f32[1,128]{1,0:T(1,128)S(1)}) %tuple.49, (f32[8,400,128]{2,1,0:T(8,128)S(1)}, ...), branch_computations={%region_3.4_spmd, %region_4.5_spmd, %region_5.6_spmd} | conditional | bytes 24 | solution.py:347
  32.5 15.2 %return_grads.5 = (f32[400,128]{1,0:T(8,128)S(1)}, f32[1,128]{1,0:T(1,128)S(1)}, f32[16,400]{1,0:T(8,128)S(1)}) custom-call(f32[8,400,128]{2,1,0:T(8,128)S(1)} %get-tuple-element.102.drhs, f32[400,128]{1,0:T(8,128)S(1)} %get-tuple-element.103.dlhs, f32[16,400]{1,0:T(8,128)S(1)} %get-tuple-element.104.drel, f32[1,128]{1,0:T(1,128)S(1)} %get-tuple-element.105.accumulator), custom_call_target="tpu_custom_call" | custom-call | tf_op jit(solution)/shard_map/cond/branch_2_fun/return_grads/pallas_call | solution.py:319
  47.6 0.7 %copy.45 = f32[128,400]{0,1:T(8,128)} copy(f32[128,400]{0,1:T(8,128)S(1)} %bitcast.11) | data formatting | bytes 409600
  48.3 0.5 %copy.46 = f32[128]{0:T(128)} copy(f32[128]{0:T(128)S(1)} %get-tuple-element.172) | data formatting | bytes 1024
  48.8 0.6 %copy.47 = f32[16,400]{1,0:T(8,128)} copy(f32[16,400]{1,0:T(8,128)S(1)} %get-tuple-element.173) | data formatting | bytes 51200
Async XLA Ops:
  0.6 31.8 %copy-start = (f32[128]{0:T(128)S(1)}, f32[128]{0:T(128)}, u32[]{:S(2)}) copy-start(f32[128]{0:T(128)} %param.16) | copy-start | bytes 1540
